TPU v7x, 128 devices: a whole 4x4x4 slice. The times are simulated.
128 devices in a mesh: row: 8 (over y, core), col: 16 (over z, x).
Axes of the slice: x: 4, y: 4, z: 4, core: 2. Of those that a mesh axis runs over, the one named last changes fastest.
Arguments:
- sigma_top: float32 [6144, 6144], P('row', 'col')
- factor_cross: float32 [6144, 6144], P('row', 'col'), may hold values from -0.078125 to 0.078125
- factor_inverse: float32 [6144, 6144], P('row', 'col')
- block_inverse: float32 [6144, 6144], P('row', 'col')
- ancestors: int32 [12], replicated, may hold values from 0 to 23, as said below
Outputs:
- sigma_cross: float32 [6144, 6144], P('row', 'col')
- sigma_child: float32 [6144, 6144], P('row', 'col')
Inputs may be any that keep to these rules, and one draw needn't show every extreme that they name: `ancestors`: 12 distinct block numbers; block 0 and block 23 are always among them.
All inputs are finite; a program needn't handle non-finite values.
Results may differ from a plain program's by a relative error of at most 0.000078.
Values sent between devices are 32-bit elements; how exact they have to be, the bound alone decides.
No kernel may reach another device: no remote copies, remote signals or barrier semaphores. Data moves between devices by JAX's collectives and lax.ppermute only.
A program may use at most 128 MiB of HBM per device.

v0:
```python
import jax
import jax.numpy as jnp
import numpy as np
from jax import lax
from jax.sharding import Mesh, PartitionSpec as P

NB = 24
NANC = 12
ROW = ("y", "core")
COL = ("z", "x")
ALL = ("y", "core", "z", "x")


def shift(x, axis, n, k):
    return lax.ppermute(x, axis, [(i, (i + k) % n) for i in range(n)])


def gather_rows(x):
    y, core = (lax.axis_index("y"), lax.axis_index("core"))
    half = x.shape[0] // 2
    left = shift(x, "y", 4, 1)
    right = shift(x, "y", 4, -1)
    far = jnp.concatenate([shift(left[:half], "y", 4, 1), shift(right[half:], "y", 4, -1)])
    mine = [x, left, right, far]
    at = [y, (y + 3) % 4, (y + 1) % 4, (y + 2) % 4]
    out = [(2 * a + core, t) for a, t in zip(at, mine)]
    out += [(2 * a + 1 - core, shift(t, "core", 2, 1)) for a, t in zip(at, mine)]
    return out


def spread(x):
    h, w = x.shape
    sub = h // 24
    return lax.all_to_all(x.reshape(3, 8, sub, w), ROW, 1, 0, tiled=True).reshape(NB, sub, w)


def pick(x, ancestors):
    return jnp.concatenate([lax.dynamic_slice_in_dim(x, ancestors[i], 1, 0) for i in range(NANC)])


def dot(a, b, dims):
    return lax.dot_general(
        a, b, (dims, ((), ())), precision=lax.Precision.HIGH, preferred_element_type=jnp.float32
    )


def per_device(sigma_top, factor_cross, factor_inverse, block_inverse, ancestors):
    h, w = sigma_top.shape
    sub = h // 24
    part = NANC * sub
    f = pick(spread(factor_cross), ancestors).reshape(part, w)
    f_all = lax.all_gather(f, COL, axis=1, tiled=True)
    strip = jnp.zeros((8 * h, w), jnp.float32)
    for r, t in gather_rows(factor_inverse):
        strip = lax.dynamic_update_slice(strip, t, (r * h, 0))
    s = pick(spread(sigma_top), ancestors).reshape(part, w)
    s_all = lax.all_gather(s, COL, axis=1, tiled=True)
    u = dot(f_all, strip, ((1,), (0,)))
    moved = lax.ppermute(
        u, ALL, [(16 * r + c, 16 * (c // 2) + 2 * r + c % 2) for r in range(8) for c in range(16)]
    )
    u_side = lax.all_gather(moved, COL, axis=0, tiled=False).reshape(8, 2, part, w)
    u_col = jnp.zeros((NANC, 8, sub, w), jnp.float32)
    for r, t in gather_rows(u):
        u_col = lax.dynamic_update_slice(u_col, t.reshape(NANC, 1, sub, w), (0, r, 0, 0))
    s_sel = jnp.concatenate(
        [lax.dynamic_slice_in_dim(s_all, ancestors[i] * 8 * sub, 8 * sub, 1) for i in range(NANC)],
        axis=1,
    )
    sigma = -dot(s_sel, u_col.reshape(8 * part, w), ((1,), (0,)))
    sigma_col = jnp.zeros((8, part, w), jnp.float32)
    for r, t in gather_rows(sigma):
        sigma_col = lax.dynamic_update_slice(sigma_col, t[None], (r, 0, 0))
    correction = jnp.concatenate([dot(u_side[:, p], sigma_col, ((0, 1), (0, 1))) for p in range(2)])
    sigma_child = block_inverse - correction
    blocks = sigma.reshape(NANC, sub, w)
    hit = ancestors[None, :] == lax.iota(jnp.int32, NB)[:, None]
    place = jnp.argmax(hit, axis=1)
    living = jnp.any(hit, axis=1)
    full = jnp.concatenate([lax.dynamic_slice_in_dim(blocks, place[b], 1, 0) for b in range(NB)])
    full = jnp.where(living[:, None, None], full, jnp.float32(0.0))
    back = lax.all_to_all(full.reshape(8, 3, sub, w), ROW, 0, 0, tiled=True)
    sigma_cross = back.reshape(8, 3, sub, w).transpose(1, 0, 2, 3).reshape(h, w)
    return (sigma_cross, sigma_child)


def solution(mesh):
    fine = Mesh(np.asarray(mesh.devices).reshape(4, 2, 4, 4), ALL)
    tile = P(ROW, COL)
    return jax.shard_map(
        per_device,
        mesh=fine,
        in_specs=(tile, tile, tile, tile, P()),
        out_specs=(tile, tile),
        check_vma=False,
    )
```

profile of v0, /device:TPU:1, one launch (start us, length us, event | category | flops | bytes accessed | tf_op | source)
XLA Modules:
  0.0 343.1 jit_solution(14482909959101323158)
XLA Ops:
  7.2 2.5 copy.63
  9.6 6.0 %all-to-all-start.1 = ((f32[3,8,32,384]{3,2,0,1:T(8,128)}), f32[3,8,32,384]{3,2,0,1:T(8,128)S(1)}, u32[]{:S(2)}, u32[]{:S(2)}) async-start(f32[3,8,32,384]{3,2,0,1:T(8,128)} %copy.63), calls=%async_computation.1 | async-start | bytes 2359296 | tf_op jit(solution)/shard_map/all_to_all | solution.py:34
  16.7 15.4 %all-to-all-done.1 = f32[3,8,32,384]{3,2,0,1:T(8,128)S(1)} async-done(((f32[3,8,32,384]{3,2,0,1:T(8,128)}), f32[3,8,32,384]{3,2,0,1:T(8,128)S(1)}, u32[]{:S(2)}, u32[]{:S(2)}) %all-to-all-start.1) | async-done | bytes 1179680 | tf_op jit(solution)/shard_map/all_to_all | solution.py:34
  32.1 4.3 %all-to-all-start = ((f32[3,8,32,384]{3,2,0,1:T(8,128)}), f32[3,8,32,384]{3,2,0,1:T(8,128)S(1)}, u32[]{:S(2)}, u32[]{:S(2)}) async-start(f32[3,8,32,384]{3,2,0,1:T(8,128)} %copy.62), calls=%async_computation | async-start | bytes 2359296 | tf_op jit(solution)/shard_map/all_to_all | solution.py:34
  64.1 26.1 %collective-permute-done = f32[768,384]{1,0:T(8,128)S(1)} collective-permute-done((f32[768,384]{1,0:T(8,128)}, f32[768,384]{1,0:T(8,128)S(1)}, u32[]{:S(2)}, u32[]{:S(2)}) %collective-permute-start) | collective-permute-done | bytes 1179680 | tf_op jit(solution)/shard_map/ppermute | solution.py:15
  90.4 2.7 collective-permute-start.3
  95.2 10.4 %collective-permute-done.2 = f32[384,384]{1,0:T(8,128)S(1)} collective-permute-done((f32[384,384]{1,0:T(8,128)S(1)}, f32[384,384]{1,0:T(8,128)S(1)}, u32[]{:S(2)}, u32[]{:S(2)}) %collective-permute-start.2) | collective-permute-done | bytes 589856 | tf_op jit(solution)/shard_map/ppermute | solution.py:15
  107.5 4.3 %broadcast_in_dim.53 = f32[6144,384]{1,0:T(8,128)} broadcast(f32[]{:T(128)} %constant.74.clone.1), dimensions={} | broadcast | bytes 9437188 | tf_op jit(solution)/shard_map/broadcast_in_dim | solution.py:53
  111.8 2.4 constant_dynamic-update-slice_fusion.69
  117.5 2.4 constant_dynamic-update-slice_fusion.65
  120.0 2.4 constant_dynamic-update-slice_fusion.64
  122.4 2.4 constant_dynamic-update-slice_fusion.63
  124.8 2.4 constant_dynamic-update-slice_fusion.62
  127.2 11.1 %all-gather.7.cloned.1.call-done = f32[384,6144]{1,0:T(8,128)} async-done(((f32[384,384]{1,0:T(8,128)}), f32[384,6144]{1,0:T(8,128)}) %all-gather.7.cloned.1.call-update) | async-done | bytes 9437200 | tf_op jit(solution)/shard_map/all_gather | solution.py:52
  138.3 11.7 %fusion.8 = f32[384,384]{1,0:T(8,128)S(1)} fusion(f32[384,6144]{1,0:T(8,128)} %all-gather.7.cloned.1.call-done, f32[6144,384]{1,0:T(8,128)} %constant_dynamic-update-slice_fusion.62), kind=kOutput, calls=%fused_computation.105 | convolution fusion | flops 5435817984 | bytes 19464192 | tf_op jit(solution)/shard_map/dot_general | solution.py:42
  150.0 5.2 %collective-permute-start.16 = (f32[384,384]{1,0:T(8,128)S(1)}, f32[384,384]{1,0:T(8,128)S(1)}, u32[]{:S(2)}, u32[]{:S(2)}) collective-permute-start(f32[384,384]{1,0:T(8,128)S(1)} %fusion.8), channel_id=1, source_target_pairs={{0,0},{1,1},{2,16},{3,17},{4,32},{5,33},{6,48},{7,49},{8,64},{9,65... | collective-permute-start | bytes 1769480 | tf_op jit(solution)/shard_map/ppermute | solution.py:59
  155.2 14.5 %collective-permute-done.16 = f32[384,384]{1,0:T(8,128)S(1)} collective-permute-done((f32[384,384]{1,0:T(8,128)S(1)}, f32[384,384]{1,0:T(8,128)S(1)}, u32[]{:S(2)}, u32[]{:S(2)}) %collective-permute-start.16) | collective-permute-done | bytes 589856 | tf_op jit(solution)/shard_map/ppermute | solution.py:59
  225.2 4.2 %collective-permute-start.8 = (f32[384,384]{1,0:T(8,128)S(1)}, f32[384,384]{1,0:T(8,128)S(1)}, u32[]{:S(2)}, u32[]{:S(2)}) collective-permute-start(f32[384,384]{1,0:T(8,128)S(1)} %fusion.8), channel_id=1, source_target_pairs={{0,32},{32,64},{64,96},{96,0},{1,33},{33,65},{65,97},{97,1},{2,34}... | collective-permute-start | bytes 1769480 | tf_op jit(solution)/shard_map/ppermute | solution.py:15
  229.4 4.4 %collective-permute-start.9 = (f32[384,384]{1,0:T(8,128)S(1)}, f32[384,384]{1,0:T(8,128)S(1)}, u32[]{:S(2)}, u32[]{:S(2)}) collective-permute-start(f32[384,384]{1,0:T(8,128)S(1)} %fusion.8), channel_id=1, source_target_pairs={{0,96},{32,0},{64,32},{96,64},{1,97},{33,1},{65,33},{97,65},{2,98}... | collective-permute-start | bytes 1769480 | tf_op jit(solution)/shard_map/ppermute | solution.py:15
  233.8 9.4 %collective-permute-start.12 = (f32[384,384]{1,0:T(8,128)S(1)}, f32[384,384]{1,0:T(8,128)S(1)}, u32[]{:S(2)}, u32[]{:S(2)}) collective-permute-start(f32[384,384]{1,0:T(8,128)S(1)} %fusion.8), channel_id=1, source_target_pairs={{0,16},{16,0},{1,17},{17,1},{2,18},{18,2},{3,19},{19,3},{4,20},{20... | collective-permute-start | bytes 1769480 | tf_op jit(solution)/shard_map/ppermute | solution.py:15
  255.5 2.7 collective-permute-start.11
  260.1 4.4 %collective-permute-done.10 = f32[192,384]{1,0:T(8,128)S(1)} collective-permute-done((f32[192,384]{1,0:T(8,128)S(1)}, f32[192,384]{1,0:T(8,128)S(1)}, u32[]{:S(2)}, u32[]{:S(2)}) %collective-permute-start.10) | collective-permute-done | bytes 294944 | tf_op jit(solution)/shard_map/ppermute | solution.py:15
  267.3 2.5 broadcast_in_dim.55
  269.8 5.0 %bitcast_dynamic-update-slice_fusion.7 = (f32[8,384,384]{2,1,0:T(8,128)}, f32[384,384]{1,0:T(8,128)S(1)}) fusion(f32[8,384,384]{2,1,0:T(8,128)} %broadcast_in_dim.55, s32[]{:T(128)S(6)} %select_n.283, f32[384,3072]{1,0:T(8,128)S(1)} %dynamic-slice_dynamic-update-slice_fusion, f32[3072,384]{1,0:T(8,128)S(1)} %bitcast.119), kind=kOutput, calls=%fused_computation.15 | convolution fusion | flops 2718056448 | bytes 10616836 | tf_op jit(solution)/shard_map/dot_general | solution.py:42
  275.4 2.9 collective-permute-start.18
  280.5 3.5 %all-to-all-start.2 = ((f32[8,3,32,384]{3,2,1,0:T(8,128)}), f32[8,3,32,384]{3,2,1,0:T(8,128)S(1)}, u32[]{:S(2)}, u32[]{:S(2)}) async-start(f32[8,3,32,384]{3,2,1,0:T(8,128)} %broadcast_select_fusion), calls=%async_computation.2 | async-start | bytes 2359296 | tf_op jit(solution)/shard_map/all_to_all | solution.py:82
  284.0 7.7 %collective-permute-done.17 = f32[384,384]{1,0:T(8,128)S(1)} collective-permute-done((f32[384,384]{1,0:T(8,128)S(1)}, f32[384,384]{1,0:T(8,128)S(1)}, u32[]{:S(2)}, u32[]{:S(2)}) %collective-permute-start.17) | collective-permute-done | bytes 589856 | tf_op jit(solution)/shard_map/ppermute | solution.py:15
  292.0 3.7 %collective-permute-start.20 = (f32[192,384]{1,0:T(8,128)S(1)}, f32[192,384]{1,0:T(8,128)S(1)}, u32[]{:S(2)}, u32[]{:S(2)}) collective-permute-start(f32[192,384]{1,0:T(8,128)S(1)} %slice.206), channel_id=1, source_target_pairs={{0,96},{32,0},{64,32},{96,64},{1,97},{33,1},{65,33},{97,65},{2,98}... | collective-permute-start | bytes 884744 | tf_op jit(solution)/shard_map/ppermute | solution.py:15
  295.8 2.2 collective-permute-start.22
  299.6 11.1 %collective-permute-done.19 = f32[192,384]{1,0:T(8,128)S(1)} collective-permute-done((f32[192,384]{1,0:T(8,128)S(1)}, f32[192,384]{1,0:T(8,128)S(1)}, u32[]{:S(2)}, u32[]{:S(2)}) %collective-permute-start.19) | collective-permute-done | bytes 294944 | tf_op jit(solution)/shard_map/ppermute | solution.py:15
  321.5 7.8 %fusion.2 = f32[384,384]{1,0:T(8,128)S(1)} fusion(f32[8,384,384]{2,1,0:T(8,128)} %bitcast_dynamic-update-slice_fusion, f32[8,2,384,384]{3,2,1,0:T(8,128)} %bitcast.120), kind=kOutput, calls=%fused_computation.4 | convolution fusion | flops 2717908992 | bytes 10027008 | tf_op jit(solution)/shard_map/dot_general | solution.py:42
  329.3 6.1 %fusion.3 = f32[384,384]{1,0:T(8,128)S(1)} fusion(f32[8,384,384]{2,1,0:T(8,128)} %bitcast_dynamic-update-slice_fusion, f32[8,2,384,384]{3,2,1,0:T(8,128)S(1)} %bitcast.121), kind=kOutput, calls=%fused_computation.5 | convolution fusion | flops 2717908992 | bytes 10027008 | tf_op jit(solution)/shard_map/dot_general | solution.py:42
  (159 shorter events, 50.5 us)
Async XLA Ops:
  7.2 29.3 %copy-start.6 = (s32[12]{0:T(128)S(1)}, s32[12]{0:T(128)}, u32[]{:S(2)}) copy-start(s32[12]{0:T(128)} %param.9) | copy-start | bytes 148
  9.6 22.5 %all-to-all-start.1 = ((f32[3,8,32,384]{3,2,0,1:T(8,128)}), f32[3,8,32,384]{3,2,0,1:T(8,128)S(1)}, u32[]{:S(2)}, u32[]{:S(2)}) async-start(f32[3,8,32,384]{3,2,0,1:T(8,128)} %copy.63), calls=%async_computation.1 | async-start | bytes 2359296 | tf_op jit(solution)/shard_map/all_to_all | solution.py:34
  32.1 26.9 %all-to-all-start = ((f32[3,8,32,384]{3,2,0,1:T(8,128)}), f32[3,8,32,384]{3,2,0,1:T(8,128)S(1)}, u32[]{:S(2)}, u32[]{:S(2)}) async-start(f32[3,8,32,384]{3,2,0,1:T(8,128)} %copy.62), calls=%async_computation | async-start | bytes 2359296 | tf_op jit(solution)/shard_map/all_to_all | solution.py:34
  36.5 101.8 %all-gather.7.cloned.1.call-start = ((), (), s32[]{:S(2)}) async-start(), calls=%async_computation.4 | async-start | bytes 10027008 | tf_op jit(solution)/shard_map/all_gather | solution.py:52
  60.2 183.0 %all-gather.5.cloned.1.call-start = ((), (), s32[]{:S(2)}) async-start(), calls=%async_computation.3 | async-start | bytes 10027008 | tf_op jit(solution)/shard_map/all_gather | solution.py:57
  61.3 260.2 %all-gather.9.cloned.1.call-start = ((), (), s32[]{:S(2)}) async-start(), calls=%async_computation.5 | async-start | bytes 10027008 | tf_op jit(solution)/shard_map/all_gather | solution.py:62
  61.3 28.9 %collective-permute-start = (f32[768,384]{1,0:T(8,128)}, f32[768,384]{1,0:T(8,128)S(1)}, u32[]{:S(2)}, u32[]{:S(2)}) collective-permute-start(f32[768,384]{1,0:T(8,128)} %param.7), channel_id=1, source_target_pairs={{0,32},{32,64},{64,96},{96,0},{1,33},{33,65},{65,97},{97,1},{2,34}... | collective-permute-start | bytes 3538952 | tf_op jit(solution)/shard_map/ppermute | solution.py:15
  62.8 27.6 %collective-permute-start.1 = (f32[768,384]{1,0:T(8,128)}, f32[768,384]{1,0:T(8,128)S(1)}, u32[]{:S(2)}, u32[]{:S(2)}) collective-permute-start(f32[768,384]{1,0:T(8,128)} %param.7), channel_id=1, source_target_pairs={{0,96},{32,0},{64,32},{96,64},{1,97},{33,1},{65,33},{97,65},{2,98}... | collective-permute-start | bytes 3538952 | tf_op jit(solution)/shard_map/ppermute | solution.py:15
  90.3 15.3 %collective-permute-start.2 = (f32[384,384]{1,0:T(8,128)S(1)}, f32[384,384]{1,0:T(8,128)S(1)}, u32[]{:S(2)}, u32[]{:S(2)}) collective-permute-start(f32[384,384]{1,0:T(8,128)S(1)} %slice.200), channel_id=1, source_target_pairs={{0,32},{32,64},{64,96},{96,0},{1,33},{33,65},{65,97},{97,1},{2,34}... | collective-permute-start | bytes 1769480 | tf_op jit(solution)/shard_map/ppermute | solution.py:15
  90.4 15.2 %collective-permute-start.3 = (f32[384,384]{1,0:T(8,128)S(1)}, f32[384,384]{1,0:T(8,128)S(1)}, u32[]{:S(2)}, u32[]{:S(2)}) collective-permute-start(f32[384,384]{1,0:T(8,128)S(1)} %slice.201), channel_id=1, source_target_pairs={{0,96},{32,0},{64,32},{96,64},{1,97},{33,1},{65,33},{97,65},{2,98}... | collective-permute-start | bytes 1769480 | tf_op jit(solution)/shard_map/ppermute | solution.py:15
  93.1 24.4 %collective-permute-start.4 = (f32[768,384]{1,0:T(8,128)}, f32[768,384]{1,0:T(8,128)}, u32[]{:S(2)}, u32[]{:S(2)}) collective-permute-start(f32[768,384]{1,0:T(8,128)} %param.7), channel_id=1, source_target_pairs={{0,16},{16,0},{1,17},{17,1},{2,18},{18,2},{3,19},{19,3},{4,20},{20... | collective-permute-start | bytes 3538952 | tf_op jit(solution)/shard_map/ppermute | solution.py:15
  94.7 25.3 %collective-permute-start.5 = (f32[768,384]{1,0:T(8,128)S(1)}, f32[768,384]{1,0:T(8,128)}, u32[]{:S(2)}, u32[]{:S(2)}) collective-permute-start(f32[768,384]{1,0:T(8,128)S(1)} %collective-permute-done), channel_id=1, source_target_pairs={{0,16},{16,0},{1,17},{17,1},{2,18},{18,2},{3,19},{19,3},{4,20},{20... | collective-permute-start | bytes 3538952 | tf_op jit(solution)/shard_map/ppermute | solution.py:15
  94.7 27.7 %collective-permute-start.6 = (f32[768,384]{1,0:T(8,128)S(1)}, f32[768,384]{1,0:T(8,128)}, u32[]{:S(2)}, u32[]{:S(2)}) collective-permute-start(f32[768,384]{1,0:T(8,128)S(1)} %collective-permute-done.1), channel_id=1, source_target_pairs={{0,16},{16,0},{1,17},{17,1},{2,18},{18,2},{3,19},{19,3},{4,20},{20... | collective-permute-start | bytes 3538952 | tf_op jit(solution)/shard_map/ppermute | solution.py:15
  105.6 19.2 %collective-permute-start.7 = (f32[768,384]{1,0:T(8,128)S(1)}, f32[768,384]{1,0:T(8,128)}, u32[]{:S(2)}, u32[]{:S(2)}) collective-permute-start(f32[768,384]{1,0:T(8,128)S(1)} %constant_dynamic-update-slice_fusion.24), channel_id=1, source_target_pairs={{0,16},{16,0},{1,17},{17,1},{2,18},{18,2},{3,19},{19,3},{4,20},{20... | collective-permute-start | bytes 3538952 | tf_op jit(solution)/shard_map/ppermute | solution.py:15
  150.0 19.7 %collective-permute-start.16 = (f32[384,384]{1,0:T(8,128)S(1)}, f32[384,384]{1,0:T(8,128)S(1)}, u32[]{:S(2)}, u32[]{:S(2)}) collective-permute-start(f32[384,384]{1,0:T(8,128)S(1)} %fusion.8), channel_id=1, source_target_pairs={{0,0},{1,1},{2,16},{3,17},{4,32},{5,33},{6,48},{7,49},{8,64},{9,65... | collective-permute-start | bytes 1769480 | tf_op jit(solution)/shard_map/ppermute | solution.py:59
  225.2 29.1 %collective-permute-start.8 = (f32[384,384]{1,0:T(8,128)S(1)}, f32[384,384]{1,0:T(8,128)S(1)}, u32[]{:S(2)}, u32[]{:S(2)}) collective-permute-start(f32[384,384]{1,0:T(8,128)S(1)} %fusion.8), channel_id=1, source_target_pairs={{0,32},{32,64},{64,96},{96,0},{1,33},{33,65},{65,97},{97,1},{2,34}... | collective-permute-start | bytes 1769480 | tf_op jit(solution)/shard_map/ppermute | solution.py:15
  229.4 26.1 %collective-permute-start.9 = (f32[384,384]{1,0:T(8,128)S(1)}, f32[384,384]{1,0:T(8,128)S(1)}, u32[]{:S(2)}, u32[]{:S(2)}) collective-permute-start(f32[384,384]{1,0:T(8,128)S(1)} %fusion.8), channel_id=1, source_target_pairs={{0,96},{32,0},{64,32},{96,64},{1,97},{33,1},{65,33},{97,65},{2,98}... | collective-permute-start | bytes 1769480 | tf_op jit(solution)/shard_map/ppermute | solution.py:15
  233.8 32.0 %collective-permute-start.12 = (f32[384,384]{1,0:T(8,128)S(1)}, f32[384,384]{1,0:T(8,128)S(1)}, u32[]{:S(2)}, u32[]{:S(2)}) collective-permute-start(f32[384,384]{1,0:T(8,128)S(1)} %fusion.8), channel_id=1, source_target_pairs={{0,16},{16,0},{1,17},{17,1},{2,18},{18,2},{3,19},{19,3},{4,20},{20... | collective-permute-start | bytes 1769480 | tf_op jit(solution)/shard_map/ppermute | solution.py:15
  254.4 10.1 %collective-permute-start.10 = (f32[192,384]{1,0:T(8,128)S(1)}, f32[192,384]{1,0:T(8,128)S(1)}, u32[]{:S(2)}, u32[]{:S(2)}) collective-permute-start(f32[192,384]{1,0:T(8,128)S(1)} %slice.202), channel_id=1, source_target_pairs={{0,32},{32,64},{64,96},{96,0},{1,33},{33,65},{65,97},{97,1},{2,34}... | collective-permute-start | bytes 884744 | tf_op jit(solution)/shard_map/ppermute | solution.py:15
  255.5 8.9 %collective-permute-start.11 = (f32[192,384]{1,0:T(8,128)S(1)}, f32[192,384]{1,0:T(8,128)S(1)}, u32[]{:S(2)}, u32[]{:S(2)}) collective-permute-start(f32[192,384]{1,0:T(8,128)S(1)} %slice.203), channel_id=1, source_target_pairs={{0,96},{32,0},{64,32},{96,64},{1,97},{33,1},{65,33},{97,65},{2,98}... | collective-permute-start | bytes 884744 | tf_op jit(solution)/shard_map/ppermute | solution.py:15
  259.3 6.5 %collective-permute-start.13 = (f32[384,384]{1,0:T(8,128)S(1)}, f32[384,384]{1,0:T(8,128)S(1)}, u32[]{:S(2)}, u32[]{:S(2)}) collective-permute-start(f32[384,384]{1,0:T(8,128)S(1)} %collective-permute-done.8), channel_id=1, source_target_pairs={{0,16},{16,0},{1,17},{17,1},{2,18},{18,2},{3,19},{19,3},{4,20},{20... | collective-permute-start | bytes 1769480 | tf_op jit(solution)/shard_map/ppermute | solution.py:15
  259.9 6.0 %collective-permute-start.14 = (f32[384,384]{1,0:T(8,128)S(1)}, f32[384,384]{1,0:T(8,128)S(1)}, u32[]{:S(2)}, u32[]{:S(2)}) collective-permute-start(f32[384,384]{1,0:T(8,128)S(1)} %collective-permute-done.9), channel_id=1, source_target_pairs={{0,16},{16,0},{1,17},{17,1},{2,18},{18,2},{3,19},{19,3},{4,20},{20... | collective-permute-start | bytes 1769480 | tf_op jit(solution)/shard_map/ppermute | solution.py:15
  264.5 2.7 collective-permute-start.15
  274.9 16.9 %collective-permute-start.17 = (f32[384,384]{1,0:T(8,128)S(1)}, f32[384,384]{1,0:T(8,128)S(1)}, u32[]{:S(2)}, u32[]{:S(2)}) collective-permute-start(f32[384,384]{1,0:T(8,128)S(1)} %get-tuple-element.41), channel_id=1, source_target_pairs={{0,32},{32,64},{64,96},{96,0},{1,33},{33,65},{65,97},{97,1},{2,34}... | collective-permute-start | bytes 1769480 | tf_op jit(solution)/shard_map/ppermute | solution.py:15
  275.4 16.7 %collective-permute-start.18 = (f32[384,384]{1,0:T(8,128)S(1)}, f32[384,384]{1,0:T(8,128)S(1)}, u32[]{:S(2)}, u32[]{:S(2)}) collective-permute-start(f32[384,384]{1,0:T(8,128)S(1)} %get-tuple-element.41), channel_id=1, source_target_pairs={{0,96},{32,0},{64,32},{96,64},{1,97},{33,1},{65,33},{97,65},{2,98}... | collective-permute-start | bytes 1769480 | tf_op jit(solution)/shard_map/ppermute | solution.py:15
  278.2 34.5 %collective-permute-start.21 = (f32[384,384]{1,0:T(8,128)S(1)}, f32[384,384]{1,0:T(8,128)}, u32[]{:S(2)}, u32[]{:S(2)}) collective-permute-start(f32[384,384]{1,0:T(8,128)S(1)} %get-tuple-element.41), channel_id=1, source_target_pairs={{0,16},{16,0},{1,17},{17,1},{2,18},{18,2},{3,19},{19,3},{4,20},{20... | collective-permute-start | bytes 1769480 | tf_op jit(solution)/shard_map/ppermute | solution.py:15
  280.5 34.1 %all-to-all-start.2 = ((f32[8,3,32,384]{3,2,1,0:T(8,128)}), f32[8,3,32,384]{3,2,1,0:T(8,128)S(1)}, u32[]{:S(2)}, u32[]{:S(2)}) async-start(f32[8,3,32,384]{3,2,1,0:T(8,128)} %broadcast_select_fusion), calls=%async_computation.2 | async-start | bytes 2359296 | tf_op jit(solution)/shard_map/all_to_all | solution.py:82
  291.8 18.9 %collective-permute-start.19 = (f32[192,384]{1,0:T(8,128)S(1)}, f32[192,384]{1,0:T(8,128)S(1)}, u32[]{:S(2)}, u32[]{:S(2)}) collective-permute-start(f32[192,384]{1,0:T(8,128)S(1)} %slice.205), channel_id=1, source_target_pairs={{0,32},{32,64},{64,96},{96,0},{1,33},{33,65},{65,97},{97,1},{2,34}... | collective-permute-start | bytes 884744 | tf_op jit(solution)/shard_map/ppermute | solution.py:15
  292.0 18.7 %collective-permute-start.20 = (f32[192,384]{1,0:T(8,128)S(1)}, f32[192,384]{1,0:T(8,128)S(1)}, u32[]{:S(2)}, u32[]{:S(2)}) collective-permute-start(f32[192,384]{1,0:T(8,128)S(1)} %slice.206), channel_id=1, source_target_pairs={{0,96},{32,0},{64,32},{96,64},{1,97},{33,1},{65,33},{97,65},{2,98}... | collective-permute-start | bytes 884744 | tf_op jit(solution)/shard_map/ppermute | solution.py:15
  295.8 20.0 %collective-permute-start.22 = (f32[384,384]{1,0:T(8,128)S(1)}, f32[384,384]{1,0:T(8,128)}, u32[]{:S(2)}, u32[]{:S(2)}) collective-permute-start(f32[384,384]{1,0:T(8,128)S(1)} %collective-permute-done.17), channel_id=1, source_target_pairs={{0,16},{16,0},{1,17},{17,1},{2,18},{18,2},{3,19},{19,3},{4,20},{20... | collective-permute-start | bytes 1769480 | tf_op jit(solution)/shard_map/ppermute | solution.py:15
  297.9 19.7 %collective-permute-start.23 = (f32[384,384]{1,0:T(8,128)S(1)}, f32[384,384]{1,0:T(8,128)}, u32[]{:S(2)}, u32[]{:S(2)}) collective-permute-start(f32[384,384]{1,0:T(8,128)S(1)} %collective-permute-done.18), channel_id=1, source_target_pairs={{0,16},{16,0},{1,17},{17,1},{2,18},{18,2},{3,19},{19,3},{4,20},{20... | collective-permute-start | bytes 1769480 | tf_op jit(solution)/shard_map/ppermute | solution.py:15
  310.8 8.8 %collective-permute-start.24 = (f32[384,384]{1,0:T(8,128)S(1)}, f32[384,384]{1,0:T(8,128)}, u32[]{:S(2)}, u32[]{:S(2)}) collective-permute-start(f32[384,384]{1,0:T(8,128)S(1)} %constant_dynamic-update-slice_fusion.52), channel_id=1, source_target_pairs={{0,16},{16,0},{1,17},{17,1},{2,18},{18,2},{3,19},{19,3},{4,20},{20... | collective-permute-start | bytes 1769480 | tf_op jit(solution)/shard_map/ppermute | solution.py:15
  (6 other events, 24.8 us)
Sparse Core Ops, SparseCore 0:
  60.3 77.9 all-gather.6
  141.0 100.0 all-gather.4
  243.3 75.4 all-gather.8
where the time goes:
time: 345 us; the launch traced here: 343 us
  waiting for transfers between devices  102 us (30%)
  between operations  89 us (26%)
  starting transfers between devices  62.1 us (18%)
  local copies, waits for them, and re-layouts  56.3 us (16%)
  matrix products  30.6 us (9%)
    ppermute x24, waiting for transfers between devices, shift(): return lax.ppermute(x, axis, [(i, (i + k) % n) for i in range(n)])  61.1 us
    ppermute x24, starting transfers between devices, shift(): return lax.ppermute(x, axis, [(i, (i + k) % n) for i in range(n)])  43.1 us
    dot_general x4, matrix products, dot(): lax.dot_general(a, b, (dims, ((), ())), precision=lax.Precision.HIGH, pre...  30.6 us
    dynamic_update_slice x8, local copies, waits for them, and re-layouts, per_device(): strip = lax.dynamic_update_slice(strip, t, (r * h, 0))  15.4 us
    all_to_all x2, waiting for transfers between devices, spread(): lax.all_to_all(x.reshape(3, 8, sub, w), ROW, 1, 0, tiled=True)  15.4 us
    unnamed x72, local copies, waits for them, and re-layouts  14.6 us
    ppermute x1, waiting for transfers between devices, per_device(): lax.ppermute(u, ALL, [(16 * r + c, 16 * (c // 2) + 2 * r + c % 2) for r i...  14.5 us
    all_gather x1, waiting for transfers between devices, per_device(): f_all = lax.all_gather(f, COL, axis=1, tiled=True)  11.1 us
  transfers between devices with their start and end apart: 31, of which 10 were waited for; matrix products, arithmetic and copies ran while one was open for 20% of the time, Pallas kernels for 0%

commit v1 on v0

--- a/solution.py
+++ b/solution.py
@@ -49,7 +49,7 @@
     sub = h // 24
     part = NANC * sub
     f = pick(spread(factor_cross), ancestors).reshape(part, w)
-    f_all = lax.all_gather(f, COL, axis=1, tiled=True)
+    f_all = jnp.concatenate(lax.all_to_all(jnp.stack([f] * lax.axis_size(COL)), COL, 0, 0), axis=1)
     strip = jnp.zeros((8 * h, w), jnp.float32)
     for r, t in gather_rows(factor_inverse):
         strip = lax.dynamic_update_slice(strip, t, (r * h, 0))

time: 345 us -> 475 us (1.38)
  waiting for transfers between devices: 102 us -> 205 us
  local copies, waits for them, and re-layouts: 56.3 us -> 68.7 us
  starting transfers between devices: 62.1 us -> 73 us
    all_to_all x0 -> x1, waiting for transfers between devices: none -> 110 us  [per_device(): lax.all_to_all(jnp.stack([f] * lax.axis_size(COL)), COL, 0, 0)]
    all_gather x1 -> x0, waiting for transfers between devices: 11.1 us -> none  [per_device(): f_all = lax.all_gather(f, COL, axis=1, tiled=True)]
    all_to_all x0 -> x1, starting transfers between devices: none -> 7.64 us  [per_device(): lax.all_to_all(jnp.stack([f] * lax.axis_size(COL)), COL, 0, 0)]
    ppermute x24, waiting for transfers between devices: 61.1 us -> 68.7 us  [shift(): return lax.ppermute(x, axis, [(i, (i + k) % n) for i in range(n)])]
    dynamic_update_slice x8, local copies, waits for them, and re-layouts: 0.46 us -> 6.95 us  [per_device(): lax.dynamic_update_slice(u_col, t.reshape(NANC, 1, sub, w), (0, r, 0, 0))]
    ppermute x24, starting transfers between devices: 43.1 us -> 49.4 us  [shift(): return lax.ppermute(x, axis, [(i, (i + k) % n) for i in range(n)])]
    another operation x0 -> x2, local copies, waits for them, and re-layouts: none -> 4.8 us  [per_device(): jnp.stack([f] * lax.axis_size(COL))]
    unnamed x72 -> x70, local copies, waits for them, and re-layouts: 14.6 us -> 13.7 us
  transfers between devices with their start and end apart: 31 -> 31, of which waited for: 10 -> 10; matrix products, arithmetic and copies ran while one was open for 20% -> 18% of each run, Pallas kernels for 0% -> 0%
where the time goes in v1:
time: 475 us; the launch traced here: 473 us
  waiting for transfers between devices  205 us (43%)
  between operations  90.3 us (19%)
  starting transfers between devices  73 us (15%)
  local copies, waits for them, and re-layouts  68.7 us (14%)
  matrix products  32.5 us (7%)
    all_to_all x1, waiting for transfers between devices, per_device(): lax.all_to_all(jnp.stack([f] * lax.axis_size(COL)), COL, 0, 0)  110 us
    ppermute x24, waiting for transfers between devices, shift(): return lax.ppermute(x, axis, [(i, (i + k) % n) for i in range(n)])  68.7 us
    ppermute x24, starting transfers between devices, shift(): return lax.ppermute(x, axis, [(i, (i + k) % n) for i in range(n)])  49.4 us
    dot_general x4, matrix products, dot(): lax.dot_general(a, b, (dims, ((), ())), precision=lax.Precision.HIGH, pre...  32.5 us
    all_to_all x2, waiting for transfers between devices, spread(): lax.all_to_all(x.reshape(3, 8, sub, w), ROW, 1, 0, tiled=True)  15.4 us
    dynamic_update_slice x8, local copies, waits for them, and re-layouts, per_device(): strip = lax.dynamic_update_slice(strip, t, (r * h, 0))  15.2 us
    unnamed x70, local copies, waits for them, and re-layouts  13.7 us
    ppermute x1, waiting for transfers between devices, per_device(): lax.ppermute(u, ALL, [(16 * r + c, 16 * (c // 2) + 2 * r + c % 2) for r i...  10.8 us
  transfers between devices with their start and end apart: 31, of which 10 were waited for; matrix products, arithmetic and copies ran while one was open for 18% of the time, Pallas kernels for 0%

profile of v1, /device:TPU:1, one launch (start us, length us, event | category | flops | bytes accessed | tf_op | source)
XLA Modules:
  0.0 472.7 jit_solution(5567941563130105688)
XLA Ops:
  7.2 2.5 copy.67
  9.6 6.0 %all-to-all-start.1 = ((f32[3,8,32,384]{3,2,0,1:T(8,128)}), f32[3,8,32,384]{3,2,0,1:T(8,128)S(1)}, u32[]{:S(2)}, u32[]{:S(2)}) async-start(f32[3,8,32,384]{3,2,0,1:T(8,128)} %copy.67), calls=%async_computation.1 | async-start | bytes 2359296 | tf_op jit(solution)/shard_map/all_to_all | solution.py:34
  16.7 15.4 %all-to-all-done.1 = f32[3,8,32,384]{3,2,0,1:T(8,128)S(1)} async-done(((f32[3,8,32,384]{3,2,0,1:T(8,128)}), f32[3,8,32,384]{3,2,0,1:T(8,128)S(1)}, u32[]{:S(2)}, u32[]{:S(2)}) %all-to-all-start.1) | async-done | bytes 1179680 | tf_op jit(solution)/shard_map/all_to_all | solution.py:34
  32.1 4.3 all-to-all-start
  61.7 4.6 stack.3
  66.2 7.6 %all-to-all-start.2 = ((f32[16,384,384]{1,2,0:T(8,128)}), f32[16,384,384]{1,2,0:T(8,128)}, u32[]{:S(2)}, u32[]{:S(2)}) async-start(f32[16,384,384]{1,2,0:T(8,128)} %stack.3), calls=%async_computation.2 | async-start | bytes 18874368 | tf_op jit(solution)/shard_map/all_to_all | solution.py:52
  76.7 25.9 %collective-permute-done = f32[768,384]{1,0:T(8,128)S(1)} collective-permute-done((f32[768,384]{1,0:T(8,128)}, f32[768,384]{1,0:T(8,128)S(1)}, u32[]{:S(2)}, u32[]{:S(2)}) %collective-permute-start) | collective-permute-done | bytes 1179680 | tf_op jit(solution)/shard_map/ppermute | solution.py:15
  102.8 2.7 collective-permute-start.3
  107.8 9.9 %collective-permute-done.2 = f32[384,384]{1,0:T(8,128)S(1)} collective-permute-done((f32[384,384]{1,0:T(8,128)S(1)}, f32[384,384]{1,0:T(8,128)S(1)}, u32[]{:S(2)}, u32[]{:S(2)}) %collective-permute-start.2) | collective-permute-done | bytes 589856 | tf_op jit(solution)/shard_map/ppermute | solution.py:15
  119.9 4.3 broadcast_in_dim.53
  124.1 2.4 constant_dynamic-update-slice_fusion.69
  129.9 2.4 constant_dynamic-update-slice_fusion.65
  132.3 2.4 constant_dynamic-update-slice_fusion.64
  134.6 2.4 constant_dynamic-update-slice_fusion.63
  137.0 2.4 constant_dynamic-update-slice_fusion.62
  139.4 110.2 %all-to-all-done.2 = f32[16,384,384]{1,2,0:T(8,128)} async-done(((f32[16,384,384]{1,2,0:T(8,128)}), f32[16,384,384]{1,2,0:T(8,128)}, u32[]{:S(2)}, u32[]{:S(2)}) %all-to-all-start.2) | async-done | bytes 9437216 | tf_op jit(solution)/shard_map/all_to_all | solution.py:52
  249.6 11.5 %fusion.8 = f32[384,384]{1,0:T(8,128)S(1)} fusion(f32[384,6144]{0,1:T(8,128)} %bitcast.27, f32[6144,384]{1,0:T(8,128)} %constant_dynamic-update-slice_fusion.62), kind=kOutput, calls=%fused_computation.105 | convolution fusion | flops 5435817984 | bytes 19464192 | tf_op jit(solution)/shard_map/dot_general | solution.py:42
  263.1 10.8 %collective-permute-done.16 = f32[384,384]{1,0:T(8,128)S(1)} collective-permute-done((f32[384,384]{1,0:T(8,128)S(1)}, f32[384,384]{1,0:T(8,128)S(1)}, u32[]{:S(2)}, u32[]{:S(2)}) %collective-permute-start.16) | collective-permute-done | bytes 589856 | tf_op jit(solution)/shard_map/ppermute | solution.py:59
  274.7 9.5 %collective-permute-start.8 = (f32[384,384]{1,0:T(8,128)S(1)}, f32[384,384]{1,0:T(8,128)S(1)}, u32[]{:S(2)}, u32[]{:S(2)}) collective-permute-start(f32[384,384]{1,0:T(8,128)S(1)} %fusion.8), channel_id=1, source_target_pairs={{0,32},{32,64},{64,96},{96,0},{1,33},{33,65},{65,97},{97,1},{2,34}... | collective-permute-start | bytes 1769480 | tf_op jit(solution)/shard_map/ppermute | solution.py:15
  287.8 11.2 %collective-permute-done.8 = f32[384,384]{1,0:T(8,128)S(1)} collective-permute-done((f32[384,384]{1,0:T(8,128)S(1)}, f32[384,384]{1,0:T(8,128)S(1)}, u32[]{:S(2)}, u32[]{:S(2)}) %collective-permute-start.8) | collective-permute-done | bytes 589856 | tf_op jit(solution)/shard_map/ppermute | solution.py:15
  352.7 13.6 %collective-permute-start.12 = (f32[384,384]{1,0:T(8,128)S(1)}, f32[384,384]{1,0:T(8,128)S(1)}, u32[]{:S(2)}, u32[]{:S(2)}) collective-permute-start(f32[384,384]{1,0:T(8,128)S(1)} %fusion.8), channel_id=1, source_target_pairs={{0,16},{16,0},{1,17},{17,1},{2,18},{18,2},{3,19},{19,3},{4,20},{20... | collective-permute-start | bytes 1769480 | tf_op jit(solution)/shard_map/ppermute | solution.py:15
  366.3 3.0 collective-permute-start.11
  369.3 2.8 broadcast_in_dim.52
  394.5 2.5 broadcast_in_dim.55
  397.0 7.1 %bitcast_dynamic-update-slice_fusion.7 = (f32[8,384,384]{2,1,0:T(8,128)}, f32[384,384]{1,0:T(8,128)S(1)}) fusion(f32[8,384,384]{2,1,0:T(8,128)} %broadcast_in_dim.55, s32[]{:T(128)S(6)} %select_n.283, f32[384,3072]{1,0:T(8,128)S(1)} %dynamic-slice_dynamic-update-slice_fusion, f32[3072,384]{1,0:T(8,128)} %bitcast.44), kind=kOutput, calls=%fused_computation.15 | convolution fusion | flops 2718056448 | bytes 10616836 | tf_op jit(solution)/shard_map/dot_general | solution.py:42
  404.1 3.4 collective-permute-start.18
  409.4 3.7 all-to-all-start.3
  413.1 8.1 %collective-permute-done.17 = f32[384,384]{1,0:T(8,128)S(1)} collective-permute-done((f32[384,384]{1,0:T(8,128)S(1)}, f32[384,384]{1,0:T(8,128)S(1)}, u32[]{:S(2)}, u32[]{:S(2)}) %collective-permute-start.17) | collective-permute-done | bytes 589856 | tf_op jit(solution)/shard_map/ppermute | solution.py:15
  421.7 3.6 collective-permute-start.20
  428.5 11.7 %collective-permute-done.19 = f32[192,384]{1,0:T(8,128)S(1)} collective-permute-done((f32[192,384]{1,0:T(8,128)S(1)}, f32[192,384]{1,0:T(8,128)S(1)}, u32[]{:S(2)}, u32[]{:S(2)}) %collective-permute-start.19) | collective-permute-done | bytes 294944 | tf_op jit(solution)/shard_map/ppermute | solution.py:15
  450.8 7.8 %fusion.2 = f32[384,384]{1,0:T(8,128)S(1)} fusion(f32[8,384,384]{2,1,0:T(8,128)} %bitcast_dynamic-update-slice_fusion, f32[8,2,384,384]{3,2,1,0:T(8,128)} %bitcast.122), kind=kOutput, calls=%fused_computation.4 | convolution fusion | flops 2717908992 | bytes 10027008 | tf_op jit(solution)/shard_map/dot_general | solution.py:42
  458.6 6.1 %fusion.3 = f32[384,384]{1,0:T(8,128)S(1)} fusion(f32[8,384,384]{2,1,0:T(8,128)} %bitcast_dynamic-update-slice_fusion, f32[8,2,384,384]{3,2,1,0:T(8,128)S(1)} %bitcast.123), kind=kOutput, calls=%fused_computation.5 | convolution fusion | flops 2717908992 | bytes 10027008 | tf_op jit(solution)/shard_map/dot_general | solution.py:42
  (158 shorter events, 60.7 us)
Async XLA Ops:
  7.2 29.3 %copy-start.5 = (s32[12]{0:T(128)S(1)}, s32[12]{0:T(128)}, u32[]{:S(2)}) copy-start(s32[12]{0:T(128)} %param.9) | copy-start | bytes 148
  9.6 22.5 %all-to-all-start.1 = ((f32[3,8,32,384]{3,2,0,1:T(8,128)}), f32[3,8,32,384]{3,2,0,1:T(8,128)S(1)}, u32[]{:S(2)}, u32[]{:S(2)}) async-start(f32[3,8,32,384]{3,2,0,1:T(8,128)} %copy.67), calls=%async_computation.1 | async-start | bytes 2359296 | tf_op jit(solution)/shard_map/all_to_all | solution.py:34
  32.1 28.0 %all-to-all-start = ((f32[3,8,32,384]{3,2,0,1:T(8,128)}), f32[3,8,32,384]{3,2,0,1:T(8,128)S(1)}, u32[]{:S(2)}, u32[]{:S(2)}) async-start(f32[3,8,32,384]{3,2,0,1:T(8,128)} %copy.66), calls=%async_computation | async-start | bytes 2359296 | tf_op jit(solution)/shard_map/all_to_all | solution.py:34
  36.5 345.5 %all-gather.4.cloned.1.call-start = ((), (), s32[]{:S(2)}) async-start(), calls=%async_computation.4 | async-start | bytes 10027008 | tf_op jit(solution)/shard_map/all_gather | solution.py:57
  66.2 183.4 %all-to-all-start.2 = ((f32[16,384,384]{1,2,0:T(8,128)}), f32[16,384,384]{1,2,0:T(8,128)}, u32[]{:S(2)}, u32[]{:S(2)}) async-start(f32[16,384,384]{1,2,0:T(8,128)} %stack.3), calls=%async_computation.2 | async-start | bytes 18874368 | tf_op jit(solution)/shard_map/all_to_all | solution.py:52
  73.9 376.9 %all-gather.6.cloned.1.call-start = ((), (), s32[]{:S(2)}) async-start(), calls=%async_computation.5 | async-start | bytes 10027008 | tf_op jit(solution)/shard_map/all_gather | solution.py:62
  73.9 28.7 %collective-permute-start = (f32[768,384]{1,0:T(8,128)}, f32[768,384]{1,0:T(8,128)S(1)}, u32[]{:S(2)}, u32[]{:S(2)}) collective-permute-start(f32[768,384]{1,0:T(8,128)} %param.7), channel_id=1, source_target_pairs={{0,32},{32,64},{64,96},{96,0},{1,33},{33,65},{65,97},{97,1},{2,34}... | collective-permute-start | bytes 3538952 | tf_op jit(solution)/shard_map/ppermute | solution.py:15
  75.4 27.4 %collective-permute-start.1 = (f32[768,384]{1,0:T(8,128)}, f32[768,384]{1,0:T(8,128)S(1)}, u32[]{:S(2)}, u32[]{:S(2)}) collective-permute-start(f32[768,384]{1,0:T(8,128)} %param.7), channel_id=1, source_target_pairs={{0,96},{32,0},{64,32},{96,64},{1,97},{33,1},{65,33},{97,65},{2,98}... | collective-permute-start | bytes 3538952 | tf_op jit(solution)/shard_map/ppermute | solution.py:15
  102.7 15.0 %collective-permute-start.2 = (f32[384,384]{1,0:T(8,128)S(1)}, f32[384,384]{1,0:T(8,128)S(1)}, u32[]{:S(2)}, u32[]{:S(2)}) collective-permute-start(f32[384,384]{1,0:T(8,128)S(1)} %slice.200), channel_id=1, source_target_pairs={{0,32},{32,64},{64,96},{96,0},{1,33},{33,65},{65,97},{97,1},{2,34}... | collective-permute-start | bytes 1769480 | tf_op jit(solution)/shard_map/ppermute | solution.py:15
  102.8 14.9 %collective-permute-start.3 = (f32[384,384]{1,0:T(8,128)S(1)}, f32[384,384]{1,0:T(8,128)S(1)}, u32[]{:S(2)}, u32[]{:S(2)}) collective-permute-start(f32[384,384]{1,0:T(8,128)S(1)} %slice.201), channel_id=1, source_target_pairs={{0,96},{32,0},{64,32},{96,64},{1,97},{33,1},{65,33},{97,65},{2,98}... | collective-permute-start | bytes 1769480 | tf_op jit(solution)/shard_map/ppermute | solution.py:15
  105.6 24.3 %collective-permute-start.4 = (f32[768,384]{1,0:T(8,128)}, f32[768,384]{1,0:T(8,128)}, u32[]{:S(2)}, u32[]{:S(2)}) collective-permute-start(f32[768,384]{1,0:T(8,128)} %param.7), channel_id=1, source_target_pairs={{0,16},{16,0},{1,17},{17,1},{2,18},{18,2},{3,19},{19,3},{4,20},{20... | collective-permute-start | bytes 3538952 | tf_op jit(solution)/shard_map/ppermute | solution.py:15
  107.3 25.0 %collective-permute-start.5 = (f32[768,384]{1,0:T(8,128)S(1)}, f32[768,384]{1,0:T(8,128)}, u32[]{:S(2)}, u32[]{:S(2)}) collective-permute-start(f32[768,384]{1,0:T(8,128)S(1)} %collective-permute-done), channel_id=1, source_target_pairs={{0,16},{16,0},{1,17},{17,1},{2,18},{18,2},{3,19},{19,3},{4,20},{20... | collective-permute-start | bytes 3538952 | tf_op jit(solution)/shard_map/ppermute | solution.py:15
  107.3 27.4 %collective-permute-start.6 = (f32[768,384]{1,0:T(8,128)S(1)}, f32[768,384]{1,0:T(8,128)}, u32[]{:S(2)}, u32[]{:S(2)}) collective-permute-start(f32[768,384]{1,0:T(8,128)S(1)} %collective-permute-done.1), channel_id=1, source_target_pairs={{0,16},{16,0},{1,17},{17,1},{2,18},{18,2},{3,19},{19,3},{4,20},{20... | collective-permute-start | bytes 3538952 | tf_op jit(solution)/shard_map/ppermute | solution.py:15
  117.8 19.2 %collective-permute-start.7 = (f32[768,384]{1,0:T(8,128)S(1)}, f32[768,384]{1,0:T(8,128)}, u32[]{:S(2)}, u32[]{:S(2)}) collective-permute-start(f32[768,384]{1,0:T(8,128)S(1)} %constant_dynamic-update-slice_fusion.24), channel_id=1, source_target_pairs={{0,16},{16,0},{1,17},{17,1},{2,18},{18,2},{3,19},{19,3},{4,20},{20... | collective-permute-start | bytes 3538952 | tf_op jit(solution)/shard_map/ppermute | solution.py:15
  261.2 12.7 %collective-permute-start.16 = (f32[384,384]{1,0:T(8,128)S(1)}, f32[384,384]{1,0:T(8,128)S(1)}, u32[]{:S(2)}, u32[]{:S(2)}) collective-permute-start(f32[384,384]{1,0:T(8,128)S(1)} %fusion.8), channel_id=1, source_target_pairs={{0,0},{1,1},{2,16},{3,17},{4,32},{5,33},{6,48},{7,49},{8,64},{9,65... | collective-permute-start | bytes 1769480 | tf_op jit(solution)/shard_map/ppermute | solution.py:59
  274.7 24.3 %collective-permute-start.8 = (f32[384,384]{1,0:T(8,128)S(1)}, f32[384,384]{1,0:T(8,128)S(1)}, u32[]{:S(2)}, u32[]{:S(2)}) collective-permute-start(f32[384,384]{1,0:T(8,128)S(1)} %fusion.8), channel_id=1, source_target_pairs={{0,32},{32,64},{64,96},{96,0},{1,33},{33,65},{65,97},{97,1},{2,34}... | collective-permute-start | bytes 1769480 | tf_op jit(solution)/shard_map/ppermute | solution.py:15
  284.2 82.2 %collective-permute-start.9 = (f32[384,384]{1,0:T(8,128)S(1)}, f32[384,384]{1,0:T(8,128)S(1)}, u32[]{:S(2)}, u32[]{:S(2)}) collective-permute-start(f32[384,384]{1,0:T(8,128)S(1)} %fusion.8), channel_id=1, source_target_pairs={{0,96},{32,0},{64,32},{96,64},{1,97},{33,1},{65,33},{97,65},{2,98}... | collective-permute-start | bytes 1769480 | tf_op jit(solution)/shard_map/ppermute | solution.py:15
  299.0 75.3 %collective-permute-start.10 = (f32[192,384]{1,0:T(8,128)S(1)}, f32[192,384]{1,0:T(8,128)S(1)}, u32[]{:S(2)}, u32[]{:S(2)}) collective-permute-start(f32[192,384]{1,0:T(8,128)S(1)} %slice.202), channel_id=1, source_target_pairs={{0,32},{32,64},{64,96},{96,0},{1,33},{33,65},{65,97},{97,1},{2,34}... | collective-permute-start | bytes 884744 | tf_op jit(solution)/shard_map/ppermute | solution.py:15
  352.7 25.8 %collective-permute-start.12 = (f32[384,384]{1,0:T(8,128)S(1)}, f32[384,384]{1,0:T(8,128)S(1)}, u32[]{:S(2)}, u32[]{:S(2)}) collective-permute-start(f32[384,384]{1,0:T(8,128)S(1)} %fusion.8), channel_id=1, source_target_pairs={{0,16},{16,0},{1,17},{17,1},{2,18},{18,2},{3,19},{19,3},{4,20},{20... | collective-permute-start | bytes 1769480 | tf_op jit(solution)/shard_map/ppermute | solution.py:15
  366.3 9.4 %collective-permute-start.11 = (f32[192,384]{1,0:T(8,128)S(1)}, f32[192,384]{1,0:T(8,128)S(1)}, u32[]{:S(2)}, u32[]{:S(2)}) collective-permute-start(f32[192,384]{1,0:T(8,128)S(1)} %slice.203), channel_id=1, source_target_pairs={{0,96},{32,0},{64,32},{96,64},{1,97},{33,1},{65,33},{97,65},{2,98}... | collective-permute-start | bytes 884744 | tf_op jit(solution)/shard_map/ppermute | solution.py:15
  372.9 6.4 %collective-permute-start.13 = (f32[384,384]{1,0:T(8,128)S(1)}, f32[384,384]{1,0:T(8,128)S(1)}, u32[]{:S(2)}, u32[]{:S(2)}) collective-permute-start(f32[384,384]{1,0:T(8,128)S(1)} %collective-permute-done.8), channel_id=1, source_target_pairs={{0,16},{16,0},{1,17},{17,1},{2,18},{18,2},{3,19},{19,3},{4,20},{20... | collective-permute-start | bytes 1769480 | tf_op jit(solution)/shard_map/ppermute | solution.py:15
  373.2 6.9 %collective-permute-start.14 = (f32[384,384]{1,0:T(8,128)S(1)}, f32[384,384]{1,0:T(8,128)S(1)}, u32[]{:S(2)}, u32[]{:S(2)}) collective-permute-start(f32[384,384]{1,0:T(8,128)S(1)} %collective-permute-done.9), channel_id=1, source_target_pairs={{0,16},{16,0},{1,17},{17,1},{2,18},{18,2},{3,19},{19,3},{4,20},{20... | collective-permute-start | bytes 1769480 | tf_op jit(solution)/shard_map/ppermute | solution.py:15
  375.8 5.2 %collective-permute-start.15 = (f32[384,384]{1,0:T(8,128)S(1)}, f32[384,384]{1,0:T(8,128)S(1)}, u32[]{:S(2)}, u32[]{:S(2)}) collective-permute-start(f32[384,384]{1,0:T(8,128)S(1)} %constant_dynamic-update-slice_fusion.26), channel_id=1, source_target_pairs={{0,16},{16,0},{1,17},{17,1},{2,18},{18,2},{3,19},{19,3},{4,20},{20... | collective-permute-start | bytes 1769480 | tf_op jit(solution)/shard_map/ppermute | solution.py:15
  404.1 17.1 %collective-permute-start.17 = (f32[384,384]{1,0:T(8,128)S(1)}, f32[384,384]{1,0:T(8,128)S(1)}, u32[]{:S(2)}, u32[]{:S(2)}) collective-permute-start(f32[384,384]{1,0:T(8,128)S(1)} %get-tuple-element.41), channel_id=1, source_target_pairs={{0,32},{32,64},{64,96},{96,0},{1,33},{33,65},{65,97},{97,1},{2,34}... | collective-permute-start | bytes 1769480 | tf_op jit(solution)/shard_map/ppermute | solution.py:15
  404.1 17.6 %collective-permute-start.18 = (f32[384,384]{1,0:T(8,128)S(1)}, f32[384,384]{1,0:T(8,128)S(1)}, u32[]{:S(2)}, u32[]{:S(2)}) collective-permute-start(f32[384,384]{1,0:T(8,128)S(1)} %get-tuple-element.41), channel_id=1, source_target_pairs={{0,96},{32,0},{64,32},{96,64},{1,97},{33,1},{65,33},{97,65},{2,98}... | collective-permute-start | bytes 1769480 | tf_op jit(solution)/shard_map/ppermute | solution.py:15
  407.5 34.5 %collective-permute-start.21 = (f32[384,384]{1,0:T(8,128)S(1)}, f32[384,384]{1,0:T(8,128)}, u32[]{:S(2)}, u32[]{:S(2)}) collective-permute-start(f32[384,384]{1,0:T(8,128)S(1)} %get-tuple-element.41), channel_id=1, source_target_pairs={{0,16},{16,0},{1,17},{17,1},{2,18},{18,2},{3,19},{19,3},{4,20},{20... | collective-permute-start | bytes 1769480 | tf_op jit(solution)/shard_map/ppermute | solution.py:15
  409.4 34.5 %all-to-all-start.3 = ((f32[8,3,32,384]{3,2,1,0:T(8,128)}), f32[8,3,32,384]{3,2,1,0:T(8,128)S(1)}, u32[]{:S(2)}, u32[]{:S(2)}) async-start(f32[8,3,32,384]{3,2,1,0:T(8,128)} %broadcast_select_fusion), calls=%async_computation.3 | async-start | bytes 2359296 | tf_op jit(solution)/shard_map/all_to_all | solution.py:82
  421.2 18.9 %collective-permute-start.19 = (f32[192,384]{1,0:T(8,128)S(1)}, f32[192,384]{1,0:T(8,128)S(1)}, u32[]{:S(2)}, u32[]{:S(2)}) collective-permute-start(f32[192,384]{1,0:T(8,128)S(1)} %slice.205), channel_id=1, source_target_pairs={{0,32},{32,64},{64,96},{96,0},{1,33},{33,65},{65,97},{97,1},{2,34}... | collective-permute-start | bytes 884744 | tf_op jit(solution)/shard_map/ppermute | solution.py:15
  421.7 18.5 %collective-permute-start.20 = (f32[192,384]{1,0:T(8,128)S(1)}, f32[192,384]{1,0:T(8,128)S(1)}, u32[]{:S(2)}, u32[]{:S(2)}) collective-permute-start(f32[192,384]{1,0:T(8,128)S(1)} %slice.206), channel_id=1, source_target_pairs={{0,96},{32,0},{64,32},{96,64},{1,97},{33,1},{65,33},{97,65},{2,98}... | collective-permute-start | bytes 884744 | tf_op jit(solution)/shard_map/ppermute | solution.py:15
  425.4 19.6 %collective-permute-start.22 = (f32[384,384]{1,0:T(8,128)S(1)}, f32[384,384]{1,0:T(8,128)}, u32[]{:S(2)}, u32[]{:S(2)}) collective-permute-start(f32[384,384]{1,0:T(8,128)S(1)} %collective-permute-done.17), channel_id=1, source_target_pairs={{0,16},{16,0},{1,17},{17,1},{2,18},{18,2},{3,19},{19,3},{4,20},{20... | collective-permute-start | bytes 1769480 | tf_op jit(solution)/shard_map/ppermute | solution.py:15
  426.8 20.1 %collective-permute-start.23 = (f32[384,384]{1,0:T(8,128)S(1)}, f32[384,384]{1,0:T(8,128)}, u32[]{:S(2)}, u32[]{:S(2)}) collective-permute-start(f32[384,384]{1,0:T(8,128)S(1)} %collective-permute-done.18), channel_id=1, source_target_pairs={{0,16},{16,0},{1,17},{17,1},{2,18},{18,2},{3,19},{19,3},{4,20},{20... | collective-permute-start | bytes 1769480 | tf_op jit(solution)/shard_map/ppermute | solution.py:15
  440.2 8.6 %collective-permute-start.24 = (f32[384,384]{1,0:T(8,128)S(1)}, f32[384,384]{1,0:T(8,128)}, u32[]{:S(2)}, u32[]{:S(2)}) collective-permute-start(f32[384,384]{1,0:T(8,128)S(1)} %constant_dynamic-update-slice_fusion.52), channel_id=1, source_target_pairs={{0,16},{16,0},{1,17},{17,1},{2,18},{18,2},{3,19},{19,3},{4,20},{20... | collective-permute-start | bytes 1769480 | tf_op jit(solution)/shard_map/ppermute | solution.py:15
  (5 other events, 24.0 us)
Sparse Core Ops, SparseCore 0:
  61.3 196.5 all-gather.3
  274.8 95.2 all-gather.5
